TPU v7x, 32 devices: a whole 2x2x4 slice. The times are simulated.
32 devices in a mesh: fsdp: 8 (over z, x), dp: 4 (over y, core).
Axes of the slice: x: 2, y: 2, z: 4, core: 2. Of those that a mesh axis runs over, the one named last changes fastest.
Arguments:
- pixels: int32 [32, 3072], P(('fsdp', 'dp')), may hold values from 0 to 255
- level_table: bfloat16 [256, 512], P('fsdp'), may hold values from -6 to 6
- channel_table: bfloat16 [3, 512], P(None, 'fsdp'), may hold values from -3 to 3
- attend_in: bfloat16 [512, 1536], P('fsdp'), may hold values from -0.25 to 0.25
- attend_out: bfloat16 [512, 512], P('fsdp'), may hold values from -1 to 1
- first_gain: bfloat16 [512], P('fsdp'), may hold values from 0.25 to 1.75
- first_bias: bfloat16 [512], P('fsdp'), may hold values from -3 to 3
- expand_weight: bfloat16 [512, 2048], P('fsdp'), may hold values from -0.25 to 0.25
- expand_bias: bfloat16 [2048], P('fsdp'), may hold values from -3 to 3
- shrink_weight: bfloat16 [2048, 512], P('fsdp'), may hold values from -0.125 to 0.125
- shrink_bias: bfloat16 [512], P('fsdp'), may hold values from -3 to 3
- second_gain: bfloat16 [512], P('fsdp'), may hold values from 0.25 to 1.75
- second_bias: bfloat16 [512], P('fsdp'), may hold values from -3 to 3
- cotangent: float32 [32, 3072, 512], P(('fsdp', 'dp')), may hold values from -6 to 6
Outputs:
- layer_out: bfloat16 [32, 3072, 512], P(('fsdp', 'dp'))
- grad_level_table: float32 [256, 512], P('fsdp')
- grad_channel_table: float32 [3, 512], P(None, 'fsdp')
- grad_attend_in: float32 [512, 1536], P('fsdp')
- grad_attend_out: float32 [512, 512], P('fsdp')
- grad_first_gain: float32 [512], P('fsdp')
- grad_first_bias: float32 [512], P('fsdp')
- grad_expand_weight: float32 [512, 2048], P('fsdp')
- grad_expand_bias: float32 [2048], P('fsdp')
- grad_shrink_weight: float32 [2048, 512], P('fsdp')
- grad_shrink_bias: float32 [512], P('fsdp')
- grad_second_gain: float32 [512], P('fsdp')
- grad_second_bias: float32 [512], P('fsdp')
All inputs are finite; a program needn't handle non-finite values.
Results may differ from a plain program's by a relative error of at most 0.012.
The roundings to bfloat16 on the way count: a program that leaves them out, or rounds other values in their place, can miss the bound.
Values may be sent and summed in bfloat16 or wider, within the bound.
A program may use at most 320 MiB of HBM per device.

v0:
```python
import functools

import jax
import jax.numpy as jnp
import numpy as np
from jax import lax
from jax.experimental import pallas as pl
from jax.experimental.pallas import tpu as pltpu
from jax.sharding import PartitionSpec as P

D = 512
HEADS = 8
HEAD_DIM = 64
FF = 2048
LEVELS = 256
CHANNELS = 3
SEQ = 3072
BLOCK = 768
BANDS = SEQ // BLOCK
PAIRS = HEADS // 2
PAIR = 2 * HEAD_DIM
REACH = 2
SUB = 256
EXTRA = 16
EPS = 1e-6
LOG2E = 1.4426950408889634
SAFE = 60.0

f32 = jnp.float32
bf16 = jnp.bfloat16
NT = (((1,), (1,)), ((), ()))
TN = (((0,), (0,)), ((), ()))
VMEM_LIMIT = 60 * 2**20


def mm(a, b):
    return jnp.dot(a, b, preferred_element_type=f32)


def mm_nt(a, b):
    return lax.dot_general(a, b, NT, preferred_element_type=f32)


def mm_tn(a, b):
    return lax.dot_general(a, b, TN, preferred_element_type=f32)


def params(*semantics):
    return pltpu.CompilerParams(
        vmem_limit_bytes=VMEM_LIMIT, dimension_semantics=semantics or None
    )


def one_hot_rows(pix):
    width = pix.shape[1]
    return (lax.broadcasted_iota(jnp.int32, (LEVELS, width), 0) == pix).astype(bf16)


def split3(x):
    hi = x.astype(bf16).astype(f32)
    rest = x - hi
    mid = rest.astype(bf16).astype(f32)
    return hi, mid, rest - mid


class Place:
    def __init__(self, ways):
        self.n = ways
        self.f = lax.axis_index("fsdp")
        self.d = lax.axis_index("dp")
        self.core = self.d % 2
        self.side = self.d // 2
        self.quarter = self.core * 2 + self.side

    def at(self, step):
        return (self.f + step) % self.n

    def to(self, step):
        return {"fsdp": self.at(step), "dp": self.d}

    def to_core(self):
        return {"fsdp": self.f, "dp": self.d + 1 - 2 * self.core}

    def to_side(self):
        return {"fsdp": self.f, "dp": self.d + 2 - 4 * self.side}

    def to_cross(self):
        return {"fsdp": self.f, "dp": 3 - self.d}

    def mates(self):
        return [self.to_core(), self.to_side(), self.to_cross()] + [self.to(step) for step in range(1, self.n)]

    def hello(self):
        barrier = pltpu.get_barrier_semaphore()
        for mate in self.mates():
            pl.semaphore_signal(barrier, inc=1, device_id=mate, device_id_type=pl.DeviceIdType.MESH)

    def greeted(self):
        pl.semaphore_wait(pltpu.get_barrier_semaphore(), self.n + 2)


def send(src, dst, sems, i, device):
    return pltpu.make_async_remote_copy(
        src_ref=src,
        dst_ref=dst,
        send_sem=sems.at[0, i],
        recv_sem=sems.at[1, i],
        device_id=device,
        device_id_type=pl.DeviceIdType.MESH,
    )


def window(which, size, count=1):
    return pl.ds(pl.multiple_of(which * size, size), size * count)


class Gather:
    def __init__(self, place, src, dst, sems, across):
        self.place, self.src, self.dst, self.sems = place, src, dst, sems
        self.across, self.n = across, place.n

    @staticmethod
    def semaphores(ways):
        return pltpu.SemaphoreType.DMA((2, 3 * ways + 1))

    def part(self, ref, f, start, count):
        if self.across is None:
            return ref.at[f]
        cut = window(start, self.dst.shape[1 + self.across] // 4, count)
        return ref.at[f, cut] if self.across == 0 else ref.at[f, :, cut]

    def mine(self):
        return self.part(self.dst, self.place.f, self.place.quarter, 1)

    def source(self):
        return self.part(self.src, 0, self.place.quarter, 1)

    def local(self):
        return pltpu.make_async_copy(self.source(), self.mine(), self.sems.at[0, 3 * self.n])

    def copy(self, step):
        return send(self.source(), self.mine(), self.sems, step, self.place.to(step))

    def side_copy(self, step):
        got = self.part(self.dst, self.place.at(self.n - step), self.place.quarter, 1)
        return send(got, got, self.sems, self.n + step, self.place.to_side())

    def core_copy(self, step):
        got = self.part(self.dst, self.place.at(self.n - step), self.place.core * 2, 2)
        return send(got, got, self.sems, 2 * self.n + step, self.place.to_core())

    def start(self):
        self.local().start()
        for step in range(1, self.n):
            self.copy(step).start()

    def swap(self, step):
        if step:
            self.copy(step).wait()
        else:
            self.local().wait()
        if self.across is not None:
            self.side_copy(step).start()

    def share(self, step):
        if self.across is not None:
            self.side_copy(step).wait()
            self.core_copy(step).start()

    def finish(self):
        if self.across is not None:
            for step in range(self.n):
                self.core_copy(step).wait()


class Reduce:
    def __init__(self, place, src, out, bufs):
        self.place, self.src, self.out, self.n = place, src, out, place.n
        self.r1, self.a1, self.r2, self.r3, self.sems = bufs
        self.size = src.shape[1] // 4

    @staticmethod
    def scratch(ways, rows, cols):
        return [
            pltpu.VMEM((ways, rows // 2, cols), bf16),
            pltpu.VMEM((ways, rows // 2, cols), bf16),
            pltpu.VMEM((ways, rows // 4, cols), bf16),
            pltpu.VMEM((ways - 1, rows // 4, cols), bf16),
            pltpu.SemaphoreType.DMA((2, ways + 5)),
        ]

    def half(self, which):
        return self.src.at[:, window(which, 2 * self.size)]

    def local(self):
        return pltpu.make_async_copy(self.half(self.place.core), self.a1, self.sems.at[0, self.n + 4])

    def core_copy(self):
        return send(self.half(1 - self.place.core), self.r1, self.sems, 0, self.place.to_core())

    def side_copy(self):
        theirs = self.a1.at[:, window(1 - self.place.side, self.size)]
        return send(theirs, self.r2, self.sems, self.n, self.place.to_side())

    def copy(self, step):
        return send(self.r2.at[self.place.at(step)], self.r3.at[step - 1], self.sems, step, self.place.to(step))

    def backs(self):
        got = self.out.at[window(self.place.quarter, self.size)]
        mates = (self.place.to_core(), self.place.to_side(), self.place.to_cross())
        return [send(got, got, self.sems, self.n + 1 + i, mate) for i, mate in enumerate(mates)]

    def start(self):
        self.core_copy().start()
        self.local().start()

    def over_sides(self):
        self.local().wait()
        self.core_copy().wait()

        @pl.loop(0, self.n)
        def _(i):
            self.a1[i] = (self.a1[i].astype(f32) + self.r1[i].astype(f32)).astype(bf16)

        self.side_copy().start()

    def over_shards(self):
        self.side_copy().wait()
        cut = window(self.place.side, self.size)

        @pl.loop(0, self.n)
        def _(i):
            self.r2[i] = (self.a1[i, cut].astype(f32) + self.r2[i].astype(f32)).astype(bf16)

        for step in range(1, self.n):
            self.copy(step).start()

    def settle(self):
        for step in range(1, self.n):
            self.copy(step).wait()
        whole = self.r2[self.place.f].astype(f32)
        for step in range(1, self.n):
            whole = whole + self.r3[step - 1].astype(f32)
        self.out[window(self.place.quarter, self.size)] = whole
        for back in self.backs():
            back.start()

    def finish(self):
        for back in self.backs():
            back.wait()

    stages = (start, over_sides, over_shards, settle, finish)


class ReduceSmall:
    def __init__(self, place, src, out, bufs):
        self.place, self.src, self.out, self.n = place, src, out, place.n
        self.r1, self.r2, self.r3, self.sems = bufs

    @staticmethod
    def scratch(ways, rows, cols):
        return [
            pltpu.VMEM((ways, rows, cols), f32),
            pltpu.VMEM((ways, rows, cols), f32),
            pltpu.VMEM((ways - 1, rows, cols), f32),
            pltpu.SemaphoreType.DMA((2, ways + 1)),
        ]

    def core_copy(self):
        return send(self.src, self.r1, self.sems, 0, self.place.to_core())

    def side_copy(self):
        return send(self.src, self.r2, self.sems, self.n, self.place.to_side())

    def copy(self, step):
        return send(self.src.at[self.place.at(step)], self.r3.at[step - 1], self.sems, step, self.place.to(step))

    def start(self):
        self.core_copy().start()

    def over_sides(self):
        self.core_copy().wait()
        self.src[...] += self.r1[...]
        self.side_copy().start()

    def over_shards(self):
        self.side_copy().wait()
        self.src[...] += self.r2[...]
        for step in range(1, self.n):
            self.copy(step).start()

    def settle(self):
        for step in range(1, self.n):
            self.copy(step).wait()
        whole = self.src[self.place.f]
        for step in range(1, self.n):
            whole = whole + self.r3[step - 1]
        self.out[...] = whole

    def finish(self):
        pass

    stages = (start, over_sides, over_shards, settle, finish)


def embed_tile(step, pix_ref, chan_ref, level, table, w, ind_ref, emb_ref, low_ref, qkv_ref, qt_ref, vt_ref, norm_ref):
    emb = mm_tn(one_hot_rows(pix_ref[...]), level) + mm_tn(chan_ref[...], table)
    emb_ref[...] = emb
    low = emb.astype(bf16)
    low_ref[...] = low
    qkv = mm(low, w)
    q = (qkv[:, :D] * HEAD_DIM**-0.5).astype(bf16)
    k = qkv[:, D : 2 * D].astype(bf16)
    v = qkv[:, 2 * D :].astype(bf16)
    qkv_ref[:, :D] = q
    qkv_ref[:, D : 2 * D] = k
    qkv_ref[:, 2 * D :] = v
    qt_ref[...] = q.T
    vt_ref[...] = v.T
    q = q.astype(f32)
    k = k.astype(f32)
    size_q = mm((q * q).astype(bf16), ind_ref[...]).max(0, keepdims=True)
    size_k = mm((k * k).astype(bf16), ind_ref[...]).max(0, keepdims=True)
    row = lax.broadcasted_iota(jnp.int32, (8, 128), 0)
    both = jnp.where(row == 0, size_q, jnp.where(row == 1, size_k, 0.0))
    norm_ref[...] = jnp.maximum(both, jnp.where(step == 0, 0.0, norm_ref[...]))


def embed_plain_kernel(pix_ref, chan_ref, level_ref, table_ref, w_ref, ind_ref, *outs):
    embed_tile(pl.program_id(0), pix_ref, chan_ref, level_ref[...], table_ref[...], w_ref[...], ind_ref, *outs)


def embed_outs():
    rows = lambda i: (i, 0)
    cols = lambda i: (0, i)
    specs = [
        pl.BlockSpec((BLOCK, D), rows),
        pl.BlockSpec((BLOCK, D), rows),
        pl.BlockSpec((BLOCK, 3 * D), rows),
        pl.BlockSpec((D, BLOCK), cols),
        pl.BlockSpec((D, BLOCK), cols),
        pl.BlockSpec((8, 128), lambda i: (0, 0)),
    ]
    shapes = [
        jax.ShapeDtypeStruct((SEQ, D), f32),
        jax.ShapeDtypeStruct((SEQ, D), bf16),
        jax.ShapeDtypeStruct((SEQ, 3 * D), bf16),
        jax.ShapeDtypeStruct((D, SEQ), bf16),
        jax.ShapeDtypeStruct((D, SEQ), bf16),
        jax.ShapeDtypeStruct((8, 128), f32),
    ]
    return specs, shapes


def head_columns():
    return (np.arange(D)[:, None] // HEAD_DIM == np.arange(128)[None, :]).astype(bf16)


def embed_plain(pix, chan, level, table, w_in):
    whole = lambda i: (0, 0)
    specs, shapes = embed_outs()
    return pl.pallas_call(
        embed_plain_kernel,
        grid=(SEQ // BLOCK,),
        in_specs=[
            pl.BlockSpec((1, BLOCK), lambda i: (0, i)),
            pl.BlockSpec((EXTRA, BLOCK), whole),
            pl.BlockSpec((LEVELS, D), whole),
            pl.BlockSpec((EXTRA, D), whole),
            pl.BlockSpec((D, 3 * D), whole),
            pl.BlockSpec((D, 128), whole),
        ],
        out_specs=specs,
        out_shape=shapes,
        compiler_params=params("arbitrary"),
    )(pix, chan, level, table, w_in, head_columns())


def half_lanes(even, odd):
    lane = lax.broadcasted_iota(jnp.int32, even.shape, 1)
    return jnp.where(lane < HEAD_DIM, even, pltpu.roll(odd, HEAD_DIM, 1))


def embed_gather_kernel(
    ways, pix_ref, chan_ref, ind_ref, level_ref, small_ref, win_ref, wo_ref,
    emb_ref, low_ref, qkv_ref, qt_ref, vt_ref, norm_ref, vec_ref, be_ref, w4_ref, wo_out,
    level_s, small_s, win_s, sem_level, sem_small, sem_in, sem_o, sem_w4,
):
    step = pl.program_id(0)
    last = SEQ // BLOCK - 1
    place = Place(ways)
    first = [
        Gather(place, small_ref, small_s, sem_small, None),
        Gather(place, level_ref, level_s, sem_level, 1),
        Gather(place, win_ref, win_s, sem_in, 0),
    ]
    later = Gather(place, wo_ref, wo_out, sem_o, 0)

    def copies():
        for i in range(3 * PAIRS):
            yield pltpu.make_async_copy(win_s.at[:, :, i * PAIR : (i + 1) * PAIR], w4_ref.at[i], sem_w4.at[i])

    @pl.when(step == 0)
    def _():
        place.hello()
        place.greeted()
        for g in (*first, later):
            g.start()
        for i in range(ways):
            for g in first:
                g.swap(i)
        for i in range(ways):
            for g in first:
                g.share(i)
        for i in range(ways // 2):
            both = [small_s[2 * i + odd].astype(f32) for odd in range(2)]
            vec_ref[:, i * 128 : (i + 1) * 128] = half_lanes(*both)
            for odd in range(2):
                for j in range(2):
                    at = ((2 * i + odd) * 2 + j) * 128
                    be_ref[0:1, at : at + 128] = both[odd][8 + j : 9 + j]
        for g in first:
            g.finish()
        for copy in copies():
            copy.start()

    table = vec_ref[...].astype(bf16)
    level = level_s[...].reshape(LEVELS, D)
    w = win_s[...].reshape(D, 3 * D)
    embed_tile(step, pix_ref, chan_ref, level, table, w, ind_ref, emb_ref, low_ref, qkv_ref, qt_ref, vt_ref, norm_ref)

    @pl.when(step == 0)
    def _():
        for i in range(ways):
            later.swap(i)

    @pl.when(step == last - 1)
    def _():
        for i in range(ways):
            later.share(i)

    @pl.when(step == last)
    def _():
        for copy in copies():
            copy.wait()
        later.finish()


def embed_gather(ways, pix, chan, level, small, w_in, wo):
    whole = lambda i: (0, 0)
    anywhere = pl.BlockSpec(memory_space=pl.ANY)
    specs, shapes = embed_outs()
    shards = [x[None] for x in (level, small, w_in, wo)]
    return pl.pallas_call(
        functools.partial(embed_gather_kernel, ways),
        grid=(SEQ // BLOCK,),
        in_specs=[
            pl.BlockSpec((1, BLOCK), lambda i: (0, i)),
            pl.BlockSpec((EXTRA, BLOCK), whole),
            pl.BlockSpec((D, 128), whole),
            *[anywhere] * 4,
        ],
        out_specs=[*specs, pl.BlockSpec((EXTRA, D), whole), pl.BlockSpec((8, FF), whole), *[anywhere] * 2],
        out_shape=[
            *shapes,
            jax.ShapeDtypeStruct((EXTRA, D), f32),
            jax.ShapeDtypeStruct((8, FF), f32),
            jax.ShapeDtypeStruct((3 * PAIRS, ways, D // ways, PAIR), bf16),
            jax.ShapeDtypeStruct((ways, *wo.shape), bf16),
        ],
        scratch_shapes=[
            *[pltpu.VMEM((ways, *x.shape), bf16) for x in (level, small, w_in)],
            *[Gather.semaphores(ways)] * 4,
            pltpu.SemaphoreType.DMA((3 * PAIRS,)),
        ],
        compiler_params=pltpu.CompilerParams(
            vmem_limit_bytes=VMEM_LIMIT, dimension_semantics=("arbitrary",), collective_id=0, has_side_effects=True
        ),
    )(pix, chan, head_columns(), *shards)


def units():
    found = []
    for band in range(BANDS):
        found += [(band, j) for j in range(max(0, band - REACH), band + 1)]
    return found


def lower_mask(keys, queries):
    key = lax.broadcasted_iota(jnp.int32, (keys, queries), 0)
    return key <= lax.broadcasted_iota(jnp.int32, (keys, queries), 1)


def spare_rows(x):
    row = lax.broadcasted_iota(jnp.int32, (HEAD_DIM, x.shape[1]), 0)
    hi, mid, low = split3(x)
    return jnp.where(row == 0, hi, jnp.where(row == 1, mid, jnp.where(row == 2, low, 0.0)))


class Fetch:
    def __init__(self, ways, sources, outs, sems):
        self.place = Place(ways)
        self.wide, self.narrow = [Gather(self.place, s, o, m, 0) for s, o, m in zip(sources, outs, sems)]

    def point(self, pair, name):
        half = self.place.n // 2
        steps_of = lambda method, parts: [functools.partial(method, i) for i in parts]
        near, far = range(half), range(half, self.place.n)
        wide, narrow = self.wide, self.narrow
        plan = {
            (0, 0): [self.place.hello],
            (0, 5): [self.place.greeted, wide.start, narrow.start],
            (1, 5): steps_of(wide.swap, near),
            (1, 9): steps_of(wide.swap, far),
            (2, 5): steps_of(narrow.swap, near),
            (2, 9): steps_of(narrow.swap, far) + steps_of(wide.share, near),
            (3, 5): steps_of(wide.share, far) + steps_of(narrow.share, near),
            (3, 9): steps_of(narrow.share, far) + [wide.finish, narrow.finish],
        }
        for (when, where), steps in plan.items():
            if where == name:

                @pl.when(pair == when)
                def _():
                    for step in steps:
                        step()


def attend_kernel(ways, linked, *refs):
    q_ref, k_ref, vt_ref, *refs = refs
    sources, refs = (refs[:2], refs[2:]) if linked else (None, refs)
    o_ref, qe_ref, *refs = refs
    outs, refs = (refs[:2], refs[2:]) if linked else (None, refs)
    acc, lsum, probs, *sems = refs
    pair = pl.program_id(0)
    fetch = Fetch(ways, sources, outs, sems) if linked else None
    lane = lax.broadcasted_iota(jnp.int32, (BLOCK, PAIR), 1)

    def head_only(q, h, other):
        mine = (lane < HEAD_DIM) if h == 0 else (lane >= HEAD_DIM)
        return jnp.where(mine, q, other)

    for unit, (band, j) in enumerate(units()):
        if linked:
            fetch.point(pair, unit)
        here = slice(band * BLOCK, (band + 1) * BLOCK)
        first = j == max(0, band - REACH)
        q = q_ref[here, :]
        off = jnp.zeros_like(q)
        tiles = [(0, BLOCK, BLOCK)] if j < band else [(t * SUB, SUB, (t + 1) * SUB) for t in range(BLOCK // SUB)]
        for h in range(2):
            qm = head_only(q, h, off)
            for at, width, count in tiles:
                ts = slice(at, at + width)
                scores = mm_nt(k_ref[j * BLOCK : j * BLOCK + count, :], qm[ts])
                p = jnp.exp2(scores * LOG2E)
                if j == band:
                    diag = jnp.where(lower_mask(SUB, SUB), p[count - SUB :], 0.0)
                    p = diag if count == SUB else jnp.concatenate([p[: count - SUB], diag], 0)
                part = p.reshape(count // 8, 8, width).sum(0)
                if not first:
                    part += lsum[h, :, ts]
                lsum[h, :, ts] = part
                probs[h, :count, ts] = p.astype(bf16)
        ext = [None, None]
        for h in range(2):
            mine = slice(h * HEAD_DIM, (h + 1) * HEAD_DIM)
            for at, width, count in tiles:
                ts = slice(at, at + width)
                out = mm(vt_ref[mine, j * BLOCK : j * BLOCK + count], probs[h, :count, ts])
                if not first:
                    out += acc[mine, ts]
                acc[mine, ts] = out
            if j == band:
                whole = lsum[h].sum(0, keepdims=True)
                acc[mine, :] = acc[mine, :] / whole
                ext[1 - h] = spare_rows(-jnp.log(whole))
        if j == band:
            o_ref[here, :] = acc[...].T.astype(bf16)
            extra = jnp.concatenate(ext, 0).T.astype(bf16)
            qe_ref[here, :PAIR] = head_only(q, 0, extra)
            qe_ref[here, PAIR:] = head_only(q, 1, extra)
    if linked:
        fetch.point(pair, len(units()))


def attend(ways, qkv, vt, shards=None):
    linked = shards is not None
    anywhere = pl.BlockSpec(memory_space=pl.ANY)
    extra, outs, sems, compiler = [], [], [], params("arbitrary")
    if linked:
        extra = [x[None] for x in shards]
        outs = [jax.ShapeDtypeStruct((ways, *x.shape), bf16) for x in shards]
        sems = [Gather.semaphores(ways)] * 2
        compiler = pltpu.CompilerParams(
            vmem_limit_bytes=VMEM_LIMIT, dimension_semantics=("arbitrary",), collective_id=2, has_side_effects=True
        )
    return pl.pallas_call(
        functools.partial(attend_kernel, ways, linked),
        grid=(PAIRS,),
        in_specs=[
            pl.BlockSpec((SEQ, PAIR), lambda p: (0, p)),
            pl.BlockSpec((SEQ, PAIR), lambda p: (0, PAIRS + p)),
            pl.BlockSpec((PAIR, SEQ), lambda p: (p, 0)),
            *[anywhere] * len(extra),
        ],
        out_specs=[
            pl.BlockSpec((SEQ, PAIR), lambda p: (0, p)),
            pl.BlockSpec((SEQ, 2 * PAIR), lambda p: (0, p)),
            *[anywhere] * len(extra),
        ],
        out_shape=[
            jax.ShapeDtypeStruct((SEQ, D), bf16),
            jax.ShapeDtypeStruct((SEQ, 2 * D), bf16),
            *outs,
        ],
        scratch_shapes=[
            pltpu.VMEM((PAIR, BLOCK), f32),
            pltpu.VMEM((2, 8, BLOCK), f32),
            pltpu.VMEM((2, BLOCK, BLOCK), bf16),
            *sems,
        ],
        compiler_params=compiler,
    )(qkv, qkv, vt, *extra)


def repair_kernel(
    norm_ref, qkv_ref, vt_ref, _att, _qe, att_ref, qe_ref, q_s, k_s, vt_s, o_s, e_s, acc, top, lsum, sems
):
    bound = jnp.max(norm_ref[0:1] * norm_ref[1:2])

    @pl.when(jnp.logical_not(bound < SAFE * SAFE))
    def _():
        lane = lax.broadcasted_iota(jnp.int32, (BLOCK, PAIR), 1)
        chunk = 128

        @pl.loop(0, PAIRS)
        def _(pair):
            at = pl.multiple_of(pair * PAIR, PAIR)
            loads = [
                pltpu.make_async_copy(qkv_ref.at[:, pl.ds(at, PAIR)], q_s, sems.at[0]),
                pltpu.make_async_copy(qkv_ref.at[:, pl.ds(pl.multiple_of(at + D, PAIR), PAIR)], k_s, sems.at[1]),
                pltpu.make_async_copy(vt_ref.at[pl.ds(at, PAIR)], vt_s, sems.at[2]),
            ]
            for load in loads:
                load.start()
            for load in loads:
                load.wait()

            @pl.loop(0, BANDS)
            def _(band):
                here = pl.ds(pl.multiple_of(band * BLOCK, BLOCK), BLOCK)
                q = q_s[here, :]
                ext = [None, None]
                begin = jnp.maximum(band - REACH, 0) * (BLOCK // chunk)
                end = (band + 1) * (BLOCK // chunk)
                for h in range(2):
                    mine = slice(h * HEAD_DIM, (h + 1) * HEAD_DIM)
                    qm = jnp.where((lane < HEAD_DIM) if h == 0 else (lane >= HEAD_DIM), q, jnp.zeros_like(q))

                    def masked(i):
                        start = pl.multiple_of(i * chunk, chunk)
                        scores = mm_nt(k_s[pl.ds(start, chunk), :], qm)
                        key = lax.broadcasted_iota(jnp.int32, scores.shape, 0) + start
                        query = lax.broadcasted_iota(jnp.int32, scores.shape, 1) + band * BLOCK
                        return start, jnp.where(key <= query, scores, -1e30)

                    top[...] = jnp.full(top.shape, -1e30, f32)
                    lsum[...] = jnp.zeros_like(lsum)
                    acc[mine] = jnp.zeros((HEAD_DIM, BLOCK), f32)

                    @pl.loop(begin, end)
                    def _(i):
                        top[...] = jnp.maximum(top[...], masked(i)[1].max(0, keepdims=True))

                    @pl.loop(begin, end)
                    def _(i):
                        start, scores = masked(i)
                        p = jnp.exp2((scores - top[0:1]) * LOG2E)
                        lsum[...] += p.reshape(chunk // 8, 8, BLOCK).sum(0)
                        acc[mine] += mm(vt_s[mine, pl.ds(start, chunk)], p.astype(bf16))

                    whole = lsum[...].sum(0, keepdims=True)
                    acc[mine] = acc[mine] / whole
                    ext[1 - h] = spare_rows(-(top[0:1] + jnp.log(whole)))
                o_s[here, :] = acc[...].T.astype(bf16)
                extra = jnp.concatenate(ext, 0).T.astype(bf16)
                e_s[here, :PAIR] = jnp.where(lane < HEAD_DIM, q, extra)
                e_s[here, PAIR:] = jnp.where(lane < HEAD_DIM, extra, q)

            stores = [
                pltpu.make_async_copy(o_s, att_ref.at[:, pl.ds(at, PAIR)], sems.at[0]),
                pltpu.make_async_copy(
                    e_s, qe_ref.at[:, pl.ds(pl.multiple_of(2 * at, 2 * PAIR), 2 * PAIR)], sems.at[1]
                ),
            ]
            for store in stores:
                store.start()
            for store in stores:
                store.wait()


def repair(sizes, qkv, vt, att, qe):
    anywhere = pl.BlockSpec(memory_space=pl.ANY)
    return pl.pallas_call(
        repair_kernel,
        in_specs=[pl.BlockSpec(memory_space=pltpu.VMEM), *[anywhere] * 4],
        out_specs=[anywhere] * 2,
        out_shape=[jax.ShapeDtypeStruct(x.shape, x.dtype) for x in (att, qe)],
        scratch_shapes=[
            pltpu.VMEM((SEQ, PAIR), bf16),
            pltpu.VMEM((SEQ, PAIR), bf16),
            pltpu.VMEM((PAIR, SEQ), bf16),
            pltpu.VMEM((SEQ, PAIR), bf16),
            pltpu.VMEM((SEQ, 2 * PAIR), bf16),
            pltpu.VMEM((PAIR, BLOCK), f32),
            pltpu.VMEM((8, BLOCK), f32),
            pltpu.VMEM((8, BLOCK), f32),
            pltpu.SemaphoreType.DMA((3,)),
        ],
        input_output_aliases={3: 0, 4: 1},
        compiler_params=params(),
    )(sizes, qkv, vt, att, qe)


def mean(x):
    return jnp.mean(x, -1, keepdims=True)


def norm(x):
    centered = x - mean(x)
    factor = lax.rsqrt(mean(centered * centered) + EPS)
    return centered * factor, factor


def norm_back(scaled, normed, factor):
    return factor * (scaled - mean(scaled) - normed * mean(scaled * normed))


def total(x):
    return x.sum(0, keepdims=True)


def middle_kernel(
    att_ref, emb_ref, cot_ref, wo_ref, we_ref, ws_ref, vec_ref, be_ref, pick_ref,
    out_ref, go_ref, de_ref, dt_ref, gwo_out, gwe_out, gws_out, gvec_ref, gbe_ref, gwo_ref, gwe_ref, gws_ref,
):
    @pl.when(pl.program_id(0) == 0)
    def _():
        for ref in (gwo_ref, gwe_ref, gws_ref, gvec_ref, gbe_ref):
            ref[...] = jnp.zeros_like(ref)

    gain1, bias1, bs, gain2, bias2 = [vec_ref[i : i + 1, :] for i in range(5)]
    att = att_ref[...]
    cot = cot_ref[...]
    normed1, factor1 = norm(emb_ref[...] + mm(att, wo_ref[...]))
    hidden = normed1 * gain1 + bias1
    low = hidden.astype(bf16)
    preact = mm(low, we_ref[...]) + be_ref[0:1, :]
    sig = jax.nn.sigmoid(preact)
    activ = (preact * sig).astype(bf16)
    slope = sig * (1.0 + preact * (1.0 - sig))
    normed2, factor2 = norm(hidden + mm(activ, ws_ref[...]) + bs)
    out_ref[...] = (normed2 * gain2 + bias2).astype(bf16)
    gtwo = norm_back(cot * gain2, normed2, factor2)
    gbranch = gtwo.astype(bf16)
    gws_ref[...] += mm_tn(activ, gbranch)
    gpre = (mm_nt(gbranch, ws_ref[...]) * slope).astype(bf16)
    gbe_ref[0:1, :] += total(gpre.astype(f32))
    gwe_ref[...] += mm_tn(low, gpre)
    ghidden = gtwo + mm_nt(gpre, we_ref[...])
    gone = norm_back(ghidden * gain1, normed1, factor1)
    go_ref[...] = gone
    gatt_branch = gone.astype(bf16)
    gwo_ref[...] += mm_tn(att, gatt_branch)
    gatt = mm_nt(gatt_branch, wo_ref[...]).astype(bf16)
    dt_ref[...] = gatt.T
    gvec_ref[0:1, :] += total(ghidden * normed1)
    gvec_ref[1:2, :] += total(ghidden)
    gvec_ref[2:3, :] += total(gbranch.astype(f32))
    gvec_ref[3:4, :] += total(cot * normed2)
    gvec_ref[4:5, :] += total(cot)

    @pl.when(pl.program_id(0) == pl.num_programs(0) - 1)
    def _():
        gwo_out[...] = gwo_ref[...].astype(bf16)
        gwe_out[...] = gwe_ref[...].astype(bf16)
        gws_out[...] = gws_ref[...].astype(bf16)

    prod = gatt.astype(f32) * att.astype(f32)
    hi, mid, _ = split3(prod)
    pick = pick_ref[...]
    half = D // 2
    place = lax.broadcasted_iota(jnp.int32, (att.shape[0], half), 1) % HEAD_DIM
    lane = lax.broadcasted_iota(jnp.int32, (att.shape[0], PAIR), 1)
    for part in range(2):
        cols = slice(part * half, (part + 1) * half)
        inner = mm(hi[:, cols].astype(bf16), pick) + mm(mid[:, cols].astype(bf16), pick)
        a, b, c = split3(inner)
        ext = jnp.where(place == 0, a, jnp.where(place == 1, b, jnp.where(place == 2, c, 0.0))).astype(bf16)
        for i in range(2):
            pair = 2 * part + i
            e = ext[:, i * PAIR : (i + 1) * PAIR]
            d = gatt[:, pair * PAIR : (pair + 1) * PAIR]
            de_ref[:, 2 * pair * PAIR : (2 * pair + 1) * PAIR] = jnp.where(lane < HEAD_DIM, d, e)
            de_ref[:, (2 * pair + 1) * PAIR : (2 * pair + 2) * PAIR] = jnp.where(lane < HEAD_DIM, e, d)


def middle(att, emb, cot, wo, we, ws, vec, be):
    tile = 768
    half = D // 2
    src = np.arange(half)[:, None] // HEAD_DIM
    dst = np.arange(half)[None, :]
    other = (dst // HEAD_DIM) ^ 1
    pick = np.where((src == other) & (dst % HEAD_DIM < 3), -1.0, 0.0).astype(bf16)
    whole = lambda i: (0, 0)
    rows = lambda i: (i, 0)
    cols = lambda i: (0, i)
    one = pl.Buffered(1)
    return pl.pallas_call(
        middle_kernel,
        grid=(SEQ // tile,),
        in_specs=[
            pl.BlockSpec((tile, D), rows),
            pl.BlockSpec((tile, D), rows),
            pl.BlockSpec((tile, D), rows),
            pl.BlockSpec((D, D), whole, pipeline_mode=one),
            pl.BlockSpec((D, FF), whole, pipeline_mode=one),
            pl.BlockSpec((FF, D), whole, pipeline_mode=one),
            pl.BlockSpec((EXTRA, D), whole),
            pl.BlockSpec((8, FF), whole),
            pl.BlockSpec((half, half), whole),
        ],
        out_specs=[
            pl.BlockSpec((tile, D), rows),
            pl.BlockSpec((tile, D), rows),
            pl.BlockSpec((tile, 2 * D), rows),
            pl.BlockSpec((D, tile), cols),
            pl.BlockSpec((D, D), whole, pipeline_mode=one),
            pl.BlockSpec((D, FF), whole, pipeline_mode=one),
            pl.BlockSpec((FF, D), whole, pipeline_mode=one),
            pl.BlockSpec((8, D), whole),
            pl.BlockSpec((8, FF), whole),
        ],
        out_shape=[
            jax.ShapeDtypeStruct((SEQ, D), bf16),
            jax.ShapeDtypeStruct((SEQ, D), f32),
            jax.ShapeDtypeStruct((SEQ, 2 * D), bf16),
            jax.ShapeDtypeStruct((D, SEQ), bf16),
            jax.ShapeDtypeStruct((D, D), bf16),
            jax.ShapeDtypeStruct((D, FF), bf16),
            jax.ShapeDtypeStruct((FF, D), bf16),
            jax.ShapeDtypeStruct((8, D), f32),
            jax.ShapeDtypeStruct((8, FF), f32),
        ],
        scratch_shapes=[pltpu.VMEM((D, D), f32), pltpu.VMEM((D, FF), f32), pltpu.VMEM((FF, D), f32)],
        compiler_params=params("arbitrary"),
    )(att, emb, cot, wo, we, ws, vec, be, pick)


def back_kernel(ways, linked, *refs):
    refs = list(refs)
    take = lambda count: [refs.pop(0) for _ in range(count)]
    qe_ref, k_ref, v_ref, de_ref, qt_ref, dt_ref, low_ref, w_ref, pix_ref, chan_ref, go_ref = take(11)
    given = take(5) if linked else None
    outs = take(6 if linked else 3)
    ke, ve, km, probs, slopes, dkt, dvt, dqa, grads, gemb, sem = take(11)
    pair = pl.program_id(0)
    copy = pltpu.make_async_copy(go_ref, gemb, sem)
    sums = Sums(ways, given, outs, refs) if linked else None

    def point(name):
        if linked:
            sums.point(pair, name)

    @pl.when(pair == 0)
    def _():
        copy.start()

    point("begin")
    lane = lax.broadcasted_iota(jnp.int32, (BLOCK, PAIR), 1)
    for band in range(BANDS):
        here = slice(band * BLOCK, (band + 1) * BLOCK)
        k = k_ref[here, :]
        v = v_ref[here, :]
        one = jnp.ones_like(k)
        zero = jnp.zeros_like(k)
        right = jnp.where(lane < HEAD_DIM + 3, one, zero)
        left = jnp.where(lane < 3, one, zero)
        ke[0, here] = jnp.where(lane < HEAD_DIM, k, right)
        ke[1, here] = jnp.where(lane < HEAD_DIM, left, k)
        ve[0, here] = jnp.where(lane < HEAD_DIM, v, right)
        ve[1, here] = jnp.where(lane < HEAD_DIM, left, v)
        km[0, here] = jnp.where(lane < HEAD_DIM, k, zero)
        km[1, here] = jnp.where(lane < HEAD_DIM, zero, k)
    for unit, (band, j) in enumerate(units()):
        point(unit)
        t0 = band * BLOCK
        k0 = j * BLOCK
        first = j == max(0, band - REACH)
        tiles = [(0, BLOCK)] if j < band else [(i * SUB, SUB) for i in range(BLOCK // SUB)]
        for h in range(2):
            mine = slice(h * HEAD_DIM, (h + 1) * HEAD_DIM)
            lanes = slice(h * PAIR, (h + 1) * PAIR)
            for at, count in tiles:
                ts = slice(t0 + at, t0 + BLOCK)
                ks = slice(k0 + at, k0 + at + count)
                scores = mm_nt(qe_ref[ts, lanes], ke[h, ks])
                p = jnp.exp2(scores * LOG2E)
                if j == band:
                    t = lax.broadcasted_iota(jnp.int32, p.shape, 0)
                    p = jnp.where(lax.broadcasted_iota(jnp.int32, p.shape, 1) <= t, p, 0.0)
                dp = mm_nt(de_ref[ts, lanes], ve[h, ks])
                cols = slice(at, at + count)
                probs[h, at:, cols] = p.astype(bf16)
                slopes[h, at:, cols] = (p * dp).astype(bf16)
        for h in range(2):
            mine = slice(h * HEAD_DIM, (h + 1) * HEAD_DIM)
            for at, count in tiles:
                ts = slice(t0 + at, t0 + BLOCK)
                ks = slice(k0 + at, k0 + at + count)
                cols = slice(at, at + count)
                dv = mm(dt_ref[mine, ts], probs[h, at:, cols])
                dk = mm(qt_ref[mine, ts], slopes[h, at:, cols])
                if j == band:
                    dvt[mine, ks] = dv
                    dkt[mine, ks] = dk
                else:
                    dvt[mine, ks] += dv
                    dkt[mine, ks] += dk
        if j < band:
            dq = mm(slopes[0], km[0, k0 : k0 + BLOCK]) + mm(slopes[1], km[1, k0 : k0 + BLOCK])
            if first:
                dqa[...] = dq
            else:
                dqa[...] += dq
        else:
            for i in range(BLOCK // SUB):
                count = (i + 1) * SUB
                rows = slice(i * SUB, count)
                dq = mm(slopes[0, rows, :count], km[0, k0 : k0 + count])
                dq += mm(slopes[1, rows, :count], km[1, k0 : k0 + count])
                if not first:
                    dq += dqa[rows]
                grads[t0 + i * SUB : t0 + count, :PAIR] = (dq * HEAD_DIM**-0.5).astype(bf16)
    for band in range(BANDS):
        here = slice(band * BLOCK, (band + 1) * BLOCK)
        grads[here, PAIR : 2 * PAIR] = dkt[:, here].T.astype(bf16)
        grads[here, 2 * PAIR :] = dvt[:, here].T.astype(bf16)

    gw = mm_tn(low_ref[...], grads[...]).astype(bf16)
    if linked:
        sums.take_pair(pair, gw)
        point("ready")
    else:
        outs[0][0] = gw

    @pl.when(pair == 0)
    def _():
        copy.wait()

    w = jnp.concatenate([w_ref[0, 0], w_ref[1, 0], w_ref[2, 0]], 1)
    for band in range(BANDS):
        here = slice(band * BLOCK, (band + 1) * BLOCK)
        gemb[here] += mm_nt(grads[here, :], w)
    point("end")

    @pl.when(pair == PAIRS - 1)
    def _():
        table = None
        for band in range(BANDS):
            here = slice(band * BLOCK, (band + 1) * BLOCK)
            rows = jnp.concatenate([one_hot_rows(pix_ref[:, here]), chan_ref[...]], 0)
            part = mm(rows, gemb[here].astype(bf16))
            table = part if band == 0 else table + part
        count = LEVELS // ways
        for f in range(ways):
            mine = table[f * count : (f + 1) * count].astype(bf16)
            to = sums.lev_src.at[f] if linked else outs[1].at[f]
            to[:count] = mine[:, : D // 2]
            to[count:] = mine[:, D // 2 :]
        if linked:
            sums.last(table[LEVELS : LEVELS + 8])
        else:
            outs[2][...] = table[LEVELS:]


def back(ways, qe, qkv, de, qt, dt, low, w4, pix, chan, gone, given=None):
    one = pl.Buffered(1)
    rows = D // ways
    linked = given is not None
    anywhere = pl.BlockSpec(memory_space=pl.ANY)
    out_specs = [
        pl.BlockSpec((1, D, 3 * PAIR), lambda p: (p, 0, 0)),
        pl.BlockSpec((ways, 2 * LEVELS // ways, D // 2), lambda p: (0, 0, 0)),
        pl.BlockSpec((EXTRA, D), lambda p: (0, 0)),
    ]
    out_shape = [
        jax.ShapeDtypeStruct((PAIRS, D, 3 * PAIR), bf16),
        jax.ShapeDtypeStruct((ways, 2 * LEVELS // ways, D // 2), bf16),
        jax.ShapeDtypeStruct((EXTRA, D), f32),
    ]
    extra, extra_specs, extra_scratch = [], [], []
    compiler = params("arbitrary")
    if linked:
        split = lambda x: x.reshape(ways, x.shape[0] // ways, x.shape[1])
        gwo, gwe, gws, gvec, gbe = given
        extra = [split(gwo), split(gwe), split(gws), gvec, gbe]
        extra_specs = [anywhere] * 3
        extra_specs += [pl.BlockSpec(x.shape, lambda p: (0, 0)) for x in (gvec, gbe)]
        shapes = [(rows, D), (rows, FF), (FF // ways, D), (rows, 3 * D), (LEVELS // ways, D), (EXTRA, 128)]
        out_specs = [pl.BlockSpec(shape, lambda p: (0, 0), pipeline_mode=one) for shape in shapes]
        out_shape = [jax.ShapeDtypeStruct(shape, f32) for shape in shapes]
        extra_scratch = Sums.scratch(ways)
        compiler = pltpu.CompilerParams(
            vmem_limit_bytes=VMEM_LIMIT, dimension_semantics=("arbitrary",), collective_id=1, has_side_effects=True
        )
    return pl.pallas_call(
        functools.partial(back_kernel, ways, linked),
        grid=(PAIRS,),
        in_specs=[
            pl.BlockSpec((SEQ, 2 * PAIR), lambda p: (0, p)),
            pl.BlockSpec((SEQ, PAIR), lambda p: (0, PAIRS + p)),
            pl.BlockSpec((SEQ, PAIR), lambda p: (0, 2 * PAIRS + p)),
            pl.BlockSpec((SEQ, 2 * PAIR), lambda p: (0, p)),
            pl.BlockSpec((PAIR, SEQ), lambda p: (p, 0)),
            pl.BlockSpec((PAIR, SEQ), lambda p: (p, 0)),
            pl.BlockSpec((SEQ, D), lambda p: (0, 0), pipeline_mode=one),
            pl.BlockSpec((3, 1, D, PAIR), lambda p: (0, p, 0, 0)),
            pl.BlockSpec((1, SEQ), lambda p: (0, 0)),
            pl.BlockSpec((EXTRA, BLOCK), lambda p: (0, 0)),
            anywhere,
            *extra_specs,
        ],
        out_specs=out_specs,
        out_shape=out_shape,
        scratch_shapes=[
            pltpu.VMEM((2, SEQ, PAIR), bf16),
            pltpu.VMEM((2, SEQ, PAIR), bf16),
            pltpu.VMEM((2, SEQ, PAIR), bf16),
            pltpu.VMEM((2, BLOCK, BLOCK), bf16),
            pltpu.VMEM((2, BLOCK, BLOCK), bf16),
            pltpu.VMEM((PAIR, SEQ), f32),
            pltpu.VMEM((PAIR, SEQ), f32),
            pltpu.VMEM((BLOCK, PAIR), f32),
            pltpu.VMEM((SEQ, 3 * PAIR), bf16),
            pltpu.VMEM((SEQ, D), f32),
            pltpu.SemaphoreType.DMA,
            *extra_scratch,
        ],
        compiler_params=compiler,
    )(qe, qkv, qkv, de, qt, dt, low, w4, pix, chan, gone, *extra)


class Sums:
    EARLY = ((0, 3), (0, "ready"), (1, "ready"), (2, "ready"), (3, 3))
    NEXT = ((0, "ready"), (1, 3), (1, "ready"), (2, "ready"), (3, "ready"))

    @staticmethod
    def sizes(ways):
        rows = D // ways
        return [(FF // ways, D), (rows, FF), (rows, D)] + [(rows, 3 * PAIR)] * PAIRS + [(2 * LEVELS // ways, D // 2)]

    @staticmethod
    def scratch(ways):
        sizes = Sums.sizes(ways)
        scratch = [pltpu.VMEM(size, f32) for size in sizes]
        scratch += [pltpu.VMEM((PAIRS, ways, *sizes[3]), bf16), pltpu.VMEM((ways, *sizes[-1]), bf16)]
        scratch += [pltpu.VMEM((ways, EXTRA, 128), f32), pltpu.VMEM((EXTRA, 128), f32)]
        for size in sizes:
            scratch += Reduce.scratch(ways, *size)
        return scratch + ReduceSmall.scratch(ways, EXTRA, 128)

    def __init__(self, ways, given, outs, scratch):
        self.ways, self.outs = ways, outs
        self.place = Place(ways)
        wo, we, ws, self.gvec, self.gbe = given
        scratch = list(scratch)
        take = lambda count: [scratch.pop(0) for _ in range(count)]
        self.results = take(4 + PAIRS)
        self.in_src, self.lev_src = take(2)
        self.small_src, self.small_out = take(2)
        sources = [ws, we, wo, *[self.in_src.at[p] for p in range(PAIRS)], self.lev_src]
        chunks = [Reduce(self.place, s, r, take(5)) for s, r in zip(sources, self.results)]
        self.early, self.pairs, self.lev = chunks[:3], chunks[3:-1], chunks[-1]
        self.small = ReduceSmall(self.place, self.small_src, self.small_out, take(4))

    def point(self, pair, name):
        @pl.when(pair == 0)
        def _():
            if name == "begin":
                self.place.hello()
            if name == 3:
                self.place.greeted()

        for stage, (when, where) in enumerate(self.EARLY):
            if where == name:

                @pl.when(pair == when)
                def _():
                    for chunk in self.early:
                        chunk.stages[stage](chunk)

        for p, chunk in reversed(list(enumerate(self.pairs))):
            for stage, (after, where) in enumerate(self.NEXT):
                if where == name and p + after < PAIRS:

                    @pl.when(pair == p + after)
                    def _():
                        chunk.stages[stage](chunk)

    def take_pair(self, pair, gw):
        self.in_src[pair] = gw.reshape(self.in_src.shape[1:])

    def last(self, channels):
        comb = self.gvec[...] + channels
        self.small_src[...] = jnp.zeros_like(self.small_src)
        for f in range(self.place.n):
            cols = comb[:, f // 2 * 128 : (f // 2 + 1) * 128]
            self.small_src[f, 0:8] = cols if f % 2 == 0 else pltpu.roll(cols, HEAD_DIM, 1)
            for j in range(2):
                at = (f * 2 + j) * 128
                self.small_src[f, 8 + j : 9 + j] = self.gbe[0:1, at : at + 128]
        done = {chunk: sum(p + after < PAIRS for after, _ in self.NEXT) for p, chunk in enumerate(self.pairs)}
        done.update({self.lev: 0, self.small: 0})
        while any(at < len(Reduce.stages) for at in done.values()):
            for chunk, at in reversed(list(done.items())):
                if at < len(Reduce.stages):
                    chunk.stages[at](chunk)
                    done[chunk] = at + 1
        o_out, e_out, s_out, in_out, lev_out, small_out = self.outs
        s_out[...], e_out[...], o_out[...] = [x[...] for x in self.results[:3]]
        for p in range(PAIRS):
            for part in range(3):
                at = (part * PAIRS + p) * PAIR
                in_out[:, at : at + PAIR] = self.results[3 + p][:, part * PAIR : (part + 1) * PAIR]
        half = lev_out.shape[0]
        lev_out[:, : D // 2] = self.results[-1][:half]
        lev_out[:, D // 2 :] = self.results[-1][half:]
        small_out[...] = self.small_out[...]


def place_kernel(o, e, s, win, lev, small, *outs):
    names = ("lev", "chan", "win", "o", "gain1", "bias1", "e", "eb", "s", "sb", "gain2", "bias2")
    to = dict(zip(names, outs))
    for name, ref in (("lev", lev), ("win", win), ("o", o), ("e", e), ("s", s)):
        to[name][...] = ref[...]
    each = to["chan"].shape[1]
    to["chan"][...] = small[5:8, :each]
    for i, name in enumerate(("gain1", "bias1", "sb", "gain2", "bias2")):
        to[name][...] = small[i : i + 1, :each]
    for i in range(2):
        to["eb"][:, i * 128 : (i + 1) * 128] = small[8 + i : 9 + i]


def place_results(ways, o, e, s, win, lev, small):
    each = D // ways
    vec = (1, each)
    shapes = [
        lev.shape, (CHANNELS, each), win.shape, o.shape, vec, vec, e.shape, (1, FF // ways), s.shape, vec, vec, vec,
    ]
    outs = pl.pallas_call(
        place_kernel,
        out_shape=[jax.ShapeDtypeStruct(shape, f32) for shape in shapes],
        compiler_params=params(),
    )(o, e, s, win, lev, small)
    return [x.reshape(-1) if x.shape[0] == 1 else x for x in outs]


def channel_rows():
    pos = np.arange(BLOCK) % CHANNELS + 5
    return (np.arange(EXTRA)[:, None] == pos[None, :]).astype(bf16)


def image(ways, pix, cot, chan, embedded, weights, shards=None):
    emb, low, qkv, qt, vt, sizes = embedded
    w4, wo, vec, be, we, ws = weights
    att, qe, *fetched = attend(ways, qkv, vt, shards)
    if shards is not None:
        we, ws = [x.reshape(-1, x.shape[2]) for x in fetched]
    att, qe = repair(sizes, qkv, vt, att, qe)
    out, gone, de, dt, *grads = middle(att, emb, cot, wo, we, ws, vec, be)
    if shards is not None:
        return out, *back(ways, qe, qkv, de, qt, dt, low, w4, pix, chan, gone, grads)
    return out, *grads, *back(ways, qe, qkv, de, qt, dt, low, w4, pix, chan, gone)


def pack_small(vectors, channels, bias):
    size = bias.shape[0] // 128
    rows = jnp.concatenate([jnp.stack(vectors), channels])
    rows = jnp.pad(rows, ((0, 0), (0, 128 - rows.shape[1])))
    return jnp.concatenate([rows, bias.reshape(size, 128), jnp.zeros((EXTRA - 8 - size, 128), bf16)])


def body(
    ways, pixels, level_table, channel_table, attend_in, attend_out, first_gain, first_bias, expand_weight,
    expand_bias, shrink_weight, shrink_bias, second_gain, second_bias, cotangent,
):
    chan = channel_rows()
    vectors = (first_gain, first_bias, shrink_bias, second_gain, second_bias)
    small = pack_small(vectors, channel_table, expand_bias)
    *embedded, vec, be, w4, wo = embed_gather(ways, pixels, chan, level_table, small, attend_in, attend_out)
    weights = (w4.reshape(3, PAIRS, D, PAIR), wo.reshape(D, D), vec, be, None, None)
    shards = (expand_weight, shrink_weight)
    out, *sums = image(ways, pixels, cotangent[0], chan, embedded, weights, shards)
    return out[None], *place_results(ways, *sums)


def plain_body(
    ways, pixels, level_table, channel_table, attend_in, attend_out, first_gain, first_bias, expand_weight,
    expand_bias, shrink_weight, shrink_bias, second_gain, second_bias, cotangent,
):
    gather = lambda x, axis=0: lax.all_gather(x, "fsdp", axis=axis, tiled=True)
    vectors = jnp.stack((first_gain, first_bias, shrink_bias, second_gain, second_bias))
    chan = channel_rows()
    small = gather(jnp.concatenate([vectors, channel_table]), 1)
    table = jnp.pad(small, ((0, EXTRA - 8), (0, 0)))
    level = gather(level_table)
    w_in = gather(attend_in)
    be = jnp.pad(gather(expand_bias).astype(f32)[None], ((0, 7), (0, 0)))
    w4 = w_in.reshape(D, 3, PAIRS, PAIR).transpose(1, 2, 0, 3)
    weights = (w4, gather(attend_out), table.astype(f32), be, gather(expand_weight), gather(shrink_weight))
    outs = []
    sums = None
    for i in range(pixels.shape[0]):
        pix = pixels[i : i + 1]
        got = image(ways, pix, cotangent[i], chan, embed_plain(pix, chan, level, table, w_in), weights)
        outs.append(got[0])
        grads = [x.astype(f32) for x in got[1:]]
        sums = grads if sums is None else [a + b for a, b in zip(sums, grads)]
    gwo, gwe, gws, gvec, gbe, gw, glev, gchan = sums
    gwin = gw.reshape(PAIRS, D, 3, PAIR).transpose(1, 2, 0, 3).reshape(D, 3 * D)
    count = LEVELS // ways
    glev = glev.reshape(ways, 2, count, D // 2).transpose(0, 2, 1, 3).reshape(LEVELS, D)

    def scatter(x, axis=0):
        return lax.psum(lax.psum_scatter(x, "fsdp", scatter_dimension=axis, tiled=True), "dp")

    small = scatter(gvec + gchan[:8], 1)
    return (
        jnp.stack(outs), scatter(glev), small[5:8], scatter(gwin), scatter(gwo), small[0], small[1], scatter(gwe),
        scatter(gbe[0]), scatter(gws), small[2], small[3], small[4],
    )


def solution(mesh):
    row = P("fsdp", None)
    vector = P("fsdp")
    shared = P(("fsdp", "dp"), None, None)
    weights = (
        row, P(None, "fsdp"), row, row, vector, vector, row, vector, row, vector, vector, vector,
    )
    ways = mesh.shape["fsdp"]
    fits = ways == 8 and mesh.shape["dp"] == 4

    def program(pixels, *rest):
        return (body if fits and pixels.shape[0] == 1 else plain_body)(ways, pixels, *rest)

    return jax.shard_map(
        program,
        mesh=mesh,
        in_specs=(P(("fsdp", "dp"), None), *weights, shared),
        out_specs=(shared, *weights),
        check_vma=False,
    )
```

profile of v0, /device:TPU:0, one launch (start us, length us, event | category | flops | bytes accessed | tf_op | source)
XLA Modules:
  0.0 592.8 jit_solution(17080110638331356360)
XLA Ops:
  0.7 0.1 pad.7.clone
  0.7 0.8 concatenate.6
  1.5 1.3 fusion.3.small_ref
  2.8 38.8 %shard_map.264 = (f32[3072,512]{1,0:T(8,128)}, bf16[3072,512]{1,0:T(8,128)(2,1)}, bf16[3072,1536]{1,0:T(8,128)(2,1)}, bf16[512,3072]{1,0:T(8,128)(2,1)}, bf16[51...) custom-call(s32[1,3072]{1,0:T(1,128)} %refs_8_.1, ...), custom_call_target="tpu_custom_call" | custom-call | tf_op jit(solution)/shard_map/pallas_call | solution.py:454
  41.7 47.0 %shard_map.265 = (bf16[3072,512]{1,0:T(8,128)(2,1)}, bf16[3072,1024]{1,0:T(8,128)(2,1)}, bf16[8,64,2048]{2,1,0:T(8,128)(2,1)}, bf16[8,256,512]{2,1,0:T(8,128)(2,1)}) custom-call(bf16[3072,1536]{1,0:T(8,128)(2,1)} %get-tuple-element.57.refs_0_.refs_1_.qkv_ref.refs_2_, bf16[3072,1536]{1,0:T(8,128)(2,1)} %get-tuple-element.57.refs_0_.refs_1_.qkv_ref.refs_2_, ...), custom_call_target="tpu_custom_call" | custom-call | tf_op jit(solution)/shard_map/pallas_call | solution.py:598
  88.7 281.0 %shard_map.266 = (bf16[3072,512]{1,0:T(8,128)(2,1)}, bf16[3072,1024]{1,0:T(8,128)(2,1)}) custom-call(f32[8,128]{1,0:T(8,128)} %get-tuple-element.56.norm_ref, bf16[3072,1536]{1,0:T(8,128)(2,1)} %get-tuple-element.57.refs_0_.refs_1_.qkv_ref.refs_2_, bf16[512,3072]{1,0:T(8,128)(2,1)} %get-tuple-element.58.refs_2_.vt_ref, ...), custom_call_target="tpu_custom_call", output_to_operand_aliasing={{0}: (3, {}), {1}: (4, {})} | custom-call | tf_op jit(solution)/shard_map/pallas_call | solution.py:705
  369.8 66.3 %shard_map.267 = (bf16[3072,512]{1,0:T(8,128)(2,1)}, f32[3072,512]{1,0:T(8,128)}, bf16[3072,1024]{1,0:T(8,128)(2,1)}, bf16[512,3072]{1,0:T(8,128)(2,1)}, bf16[51...) custom-call(bf16[3072,512]{1,0:T(8,128)(2,1)} %get-tuple-element.61., ...), custom_call_target="tpu_custom_call" | custom-call | tf_op jit(solution)/shard_map/pallas_call | solution.py:820
  436.0 153.8 %shard_map.268 = (f32[64,512]{1,0:T(8,128)}, f32[64,2048]{1,0:T(8,128)}, f32[256,512]{1,0:T(8,128)}, f32[64,1536]{1,0:T(8,128)}, f32[32,512]{1,0:T(8,128)}, /*index=5*/f32[16,128]{1,0:T(8,128)}) custom-call(bf16[3072,1024]{1,0:T(8,128)(2,1)} %get-tuple-element.69.refs_0_, bf16[3072,1536]{1,0:T(8,128)(2,1)} %get-tuple-element.57.refs_0_.refs_1_.qkv_ref.refs_2_, ...), custom_call_target="tpu_custom_call" | custom-call | tf_op jit(solution)/shard_map/pallas_call | solution.py:1018
  589.9 2.6 shard_map.269
  (1 shorter events, 0.0 us)
where the time goes:
time: 602 us; the launch traced here: 593 us
  Pallas kernels  590 us (98%)
    pallas_call x1, Pallas kernels, repair(): pl.pallas_call(repair_kernel, in_specs=[pl.BlockSpec(memory_space=pltpu.V...  281 us
    pallas_call x1, Pallas kernels, back(): pl.pallas_call(functools.partial(back_kernel, ways, linked), grid=(PAIRS,...  154 us
    pallas_call x1, Pallas kernels, middle(): pl.pallas_call(middle_kernel, grid=(SEQ // tile,), in_specs=[pl.BlockSpec...  66.3 us
    pallas_call x1, Pallas kernels, attend(): pl.pallas_call(functools.partial(attend_kernel, ways, linked), grid=(PAIR...  47 us
    pallas_call x1, Pallas kernels, embed_gather(): pl.pallas_call(functools.partial(embed_gather_kernel, ways), grid=(SEQ //...  38.8 us

commit v1 on v0

--- a/solution.py
+++ b/solution.py
@@ -510,9 +510,10 @@
         plan = {
             (0, 0): [self.place.hello],
             (0, 5): [self.place.greeted, wide.start, narrow.start],
-            (1, 5): steps_of(wide.swap, near),
+            (0, 9): [functools.partial(wide.swap, 0), functools.partial(narrow.swap, 0)],
+            (1, 5): steps_of(wide.swap, near[1:]),
             (1, 9): steps_of(wide.swap, far),
-            (2, 5): steps_of(narrow.swap, near),
+            (2, 5): steps_of(narrow.swap, near[1:]),
             (2, 9): steps_of(narrow.swap, far) + steps_of(wide.share, near),
             (3, 5): steps_of(wide.share, far) + steps_of(narrow.share, near),
             (3, 9): steps_of(narrow.share, far) + [wide.finish, narrow.finish],

time: 602 us -> 602 us (level)
  no operation moved by 1% of the time
where the time goes in v1:
time: 602 us; the launch traced here: 593 us
  Pallas kernels  590 us (98%)
    pallas_call x1, Pallas kernels, repair(): pl.pallas_call(repair_kernel, in_specs=[pl.BlockSpec(memory_space=pltpu.V...  281 us
    pallas_call x1, Pallas kernels, back(): pl.pallas_call(functools.partial(back_kernel, ways, linked), grid=(PAIRS,...  154 us
    pallas_call x1, Pallas kernels, middle(): pl.pallas_call(middle_kernel, grid=(SEQ // tile,), in_specs=[pl.BlockSpec...  66.3 us
    pallas_call x1, Pallas kernels, attend(): pl.pallas_call(functools.partial(attend_kernel, ways, linked), grid=(PAIR...  47.1 us
    pallas_call x1, Pallas kernels, embed_gather(): pl.pallas_call(functools.partial(embed_gather_kernel, ways), grid=(SEQ //...  38.8 us

profile of v1, /device:TPU:0, one launch (start us, length us, event | category | flops | bytes accessed | tf_op | source)
XLA Modules:
  0.0 592.9 jit_solution(8049758958195877254)
XLA Ops:
  0.7 0.1 pad.7.clone
  0.7 0.8 concatenate.6
  1.5 1.3 fusion.3.small_ref
  2.8 38.8 %shard_map.264 = (f32[3072,512]{1,0:T(8,128)}, bf16[3072,512]{1,0:T(8,128)(2,1)}, bf16[3072,1536]{1,0:T(8,128)(2,1)}, bf16[512,3072]{1,0:T(8,128)(2,1)}, bf16[51...) custom-call(s32[1,3072]{1,0:T(1,128)} %refs_8_.1, ...), custom_call_target="tpu_custom_call" | custom-call | tf_op jit(solution)/shard_map/pallas_call | solution.py:454
  41.7 47.1 %shard_map.265 = (bf16[3072,512]{1,0:T(8,128)(2,1)}, bf16[3072,1024]{1,0:T(8,128)(2,1)}, bf16[8,64,2048]{2,1,0:T(8,128)(2,1)}, bf16[8,256,512]{2,1,0:T(8,128)(2,1)}) custom-call(bf16[3072,1536]{1,0:T(8,128)(2,1)} %get-tuple-element.57.refs_0_.refs_1_.qkv_ref.refs_2_, bf16[3072,1536]{1,0:T(8,128)(2,1)} %get-tuple-element.57.refs_0_.refs_1_.qkv_ref.refs_2_, ...), custom_call_target="tpu_custom_call" | custom-call | tf_op jit(solution)/shard_map/pallas_call | solution.py:599
  88.8 281.0 %shard_map.266 = (bf16[3072,512]{1,0:T(8,128)(2,1)}, bf16[3072,1024]{1,0:T(8,128)(2,1)}) custom-call(f32[8,128]{1,0:T(8,128)} %get-tuple-element.56.norm_ref, bf16[3072,1536]{1,0:T(8,128)(2,1)} %get-tuple-element.57.refs_0_.refs_1_.qkv_ref.refs_2_, bf16[512,3072]{1,0:T(8,128)(2,1)} %get-tuple-element.58.refs_2_.vt_ref, ...), custom_call_target="tpu_custom_call", output_to_operand_aliasing={{0}: (3, {}), {1}: (4, {})} | custom-call | tf_op jit(solution)/shard_map/pallas_call | solution.py:706
  369.8 66.3 %shard_map.267 = (bf16[3072,512]{1,0:T(8,128)(2,1)}, f32[3072,512]{1,0:T(8,128)}, bf16[3072,1024]{1,0:T(8,128)(2,1)}, bf16[512,3072]{1,0:T(8,128)(2,1)}, bf16[51...) custom-call(bf16[3072,512]{1,0:T(8,128)(2,1)} %get-tuple-element.61., ...), custom_call_target="tpu_custom_call" | custom-call | tf_op jit(solution)/shard_map/pallas_call | solution.py:821
  436.1 153.8 %shard_map.268 = (f32[64,512]{1,0:T(8,128)}, f32[64,2048]{1,0:T(8,128)}, f32[256,512]{1,0:T(8,128)}, f32[64,1536]{1,0:T(8,128)}, f32[32,512]{1,0:T(8,128)}, /*index=5*/f32[16,128]{1,0:T(8,128)}) custom-call(bf16[3072,1024]{1,0:T(8,128)(2,1)} %get-tuple-element.69.refs_0_, bf16[3072,1536]{1,0:T(8,128)(2,1)} %get-tuple-element.57.refs_0_.refs_1_.qkv_ref.refs_2_, ...), custom_call_target="tpu_custom_call" | custom-call | tf_op jit(solution)/shard_map/pallas_call | solution.py:1019
  590.0 2.6 shard_map.269
  (1 shorter events, 0.0 us)
